TPU v7x, 32 devices: a whole 2x2x4 slice. The times are simulated.
32 devices in a mesh: parts: 2 (over y), dp: 4 (over z), layer: 2 (over x), module: 2 (over core).
Axes of the slice: x: 2, y: 2, z: 4, core: 2. Of those that a mesh axis runs over, the one named last changes fastest.
Arguments:
- train_acts: bfloat16 [8, 128, 32, 1024], P(('layer', 'module'), ('parts', 'dp')), parts along dimension 1, may hold values from -6 to 6
- train_grads: bfloat16 [8, 128, 32, 1024], P(('layer', 'module'), ('parts', 'dp')), parts along dimension 1, may hold values from -6 to 6
- lengths: int32 [128], P(('parts', 'dp')), parts along dimension 0, may hold values from 256 to 1024
- query_grads: bfloat16 [1024, 8, 1024], P(('parts', 'dp'), ('layer', 'module')), parts along dimension 0, may hold values from -0.0078125 to 0.0078125
- inv_in: float32 [8, 32, 32], P(('layer', 'module')), may hold values from -1 to 4, as said below
- inv_out: float32 [8, 32, 32], P(('layer', 'module')), may hold values from -1 to 4, as said below
- query_ids: int32 [1024], P('parts'), parts along dimension 0, may hold values from 0 to 63
Outputs:
- influence: float32 [128, 512], P(('parts', 'dp'), ('layer', 'module')), parts along dimension 0
There are 2 independent parts, one for each index of `parts`. A program takes and returns all parts, laid end to end along the dimension named above; an argument that names none is the same for every part. Nothing has to cross between parts.
Inputs may be any that keep to these rules, and one draw needn't show every extreme that they name: `inv_in`: symmetric. `inv_out`: symmetric.
All inputs are finite; a program needn't handle non-finite values.
Results may differ from a plain program's by a relative error of at most 0.0041.
Values may be sent and summed in bfloat16 or wider, within the bound.
A program may use at most 64 MiB of HBM per device.

v0:
```python
import jax
import jax.numpy as jnp
from jax import lax
from jax.sharding import PartitionSpec as P


def on_device(train_acts, train_grads, lengths, query_grads, inv_in, inv_out, query_ids):
    mod_dev, ex_dev, rank_size, seq_len = train_acts.shape
    flat_width = mod_dev * rank_size * rank_size
    positions = lax.broadcasted_iota(jnp.int32, (ex_dev, seq_len), 1)
    keep_mask = (positions < lengths[:, None]).astype(jnp.bfloat16)
    masked = train_grads * keep_mask[None, :, None, :]
    outer_sum = jnp.einsum(
        "mnot,mnit->nmoi", masked, train_acts, preferred_element_type=jnp.float32
    )
    example_grads = outer_sum.astype(jnp.bfloat16).reshape(ex_dev, flat_width)
    local_queries = query_grads.shape[0]
    raw_queries = query_grads.astype(jnp.float32).reshape(
        local_queries, mod_dev, rank_size, rank_size
    )
    half_done = jnp.einsum("mab,qmbc->qmac", inv_out, raw_queries, precision=lax.Precision.HIGHEST)
    full_done = jnp.einsum("qmac,mcd->qmad", half_done, inv_in, precision=lax.Precision.HIGHEST)
    precond = full_done.astype(jnp.bfloat16).reshape(local_queries, flat_width)
    dp_index = lax.axis_index("dp")
    dp_size = lax.axis_size("dp")
    lm_index = lax.axis_index(("layer", "module"))
    lm_size = lax.axis_size(("layer", "module"))
    queries_all = local_queries * dp_size
    owned_cols = queries_all // lm_size
    partial_value = jnp.einsum(
        "nk,qk->nq",
        example_grads,
        lax.all_gather(precond, "dp", axis=0, tiled=True),
        preferred_element_type=jnp.float32,
    )
    owned_scores = lax.psum_scatter(
        partial_value, ("layer", "module"), scatter_dimension=1, tiled=True
    )
    row_index = dp_index * ex_dev + lax.broadcasted_iota(jnp.int32, (ex_dev, owned_cols), 0)
    own_ids = lax.dynamic_slice_in_dim(query_ids, lm_index * owned_cols, owned_cols, 0)
    same = row_index == own_ids[None, :]
    return jnp.where(same, jnp.zeros_like(owned_scores), owned_scores)


def solution(mesh):
    return jax.shard_map(
        on_device,
        mesh=mesh,
        in_specs=(
            P(("layer", "module"), ("parts", "dp"), None, None),
            P(("layer", "module"), ("parts", "dp"), None, None),
            P(("parts", "dp")),
            P(("parts", "dp"), ("layer", "module"), None),
            P(("layer", "module"), None, None),
            P(("layer", "module"), None, None),
            P("parts"),
        ),
        out_specs=P(("parts", "dp"), ("layer", "module")),
        check_vma=False,
    )
```

profile of v0, /device:TPU:1, one launch (start us, length us, event | category | flops | bytes accessed | tf_op | source)
XLA Modules:
  0.0 88.6 jit_solution(12208760459170750422)
XLA Ops:
  6.5 0.0 copy-start
  6.5 0.0 copy-start.1
  6.5 0.0 all-gather.2.cloned.1.call-start
  6.5 1.6 %copy.13 = bf16[128,2,1024]{0,2,1:T(8,128)(2,1)S(1)} copy(bf16[128,2,1024]{2,1,0:T(2,128)(2,1)} %param.10) | data formatting | bytes 1048576 | tf_op args[3]
  8.1 0.0 copy-start.2
  8.1 1.3 %fusion.10 = f32[2,128,32,32]{1,3,2,0:T(8,128)S(1)} fusion(bf16[128,2,32,32]{0,3,2,1:T(8,128)(2,1)S(1)} %bitcast.22, f32[2,32,32]{2,1,0:T(8,128)} %param.12), kind=kOutput, calls=%fused_computation.8 | convolution fusion | flops 100663296 | bytes 1581056 | tf_op jit(solution)/shard_map/mab,qmbc->qmac/dot_general | solution.py:21
  9.5 0.0 copy-done.1
  9.5 2.5 %convolution_convert_fusion = bf16[2,128,32,32]{1,3,2,0:T(8,128)(2,1)} fusion(f32[2,128,32,32]{1,3,2,0:T(8,128)S(1)} %fusion.10, f32[2,32,32]{2,1,0:T(8,128)S(1)} %copy-done.1), kind=kOutput, calls=%fused_computation.3 | convolution fusion | flops 100925440 | bytes 1581056 | tf_op jit(solution)/shard_map/qmac,mcd->qmad/dot_general | solution.py:22
  12.0 0.0 all-gather.2.cloned.1.call-update
  12.0 0.0 reduce-scatter.2.cloned.1.call-start
  12.1 0.0 copy-done.2
  12.1 0.1 fusion.12
  12.2 0.0 copy-done
  12.2 2.3 %fusion.3 = bf16[16,2,32,32]{3,2,1,0:T(8,128)(2,1)S(1)} fusion(bf16[2,16,32,1024]{3,2,1,0:T(8,128)(2,1)S(1)} %copy-done, bf16[2,16,32,1024]{3,2,1,0:T(8,128)(2,1)} %param.8, bf16[16,1024]{1,0:T(8,128)(2,1)S(1)} %fusion.12), kind=kOutput, calls=%fused_computation.4 | convolution fusion | flops 68190208 | bytes 4292608 | tf_op jit(solution)/shard_map/mnot,mnit->nmoi/dot_general | solution.py:13
  14.4 0.3 reshape.26
  14.7 0.8 dynamic_slice.3
  15.5 44.3 %all-gather.2.cloned.1.call-done = bf16[512,2048]{0,1:T(8,128)(2,1)} async-done(((bf16[128,2048]{0,1:T(8,128)(2,1)}), bf16[512,2048]{0,1:T(8,128)(2,1)}) %all-gather.2.cloned.1.call-update) | async-done | bytes 2097168 | tf_op jit(solution)/shard_map/all_gather | solution.py:33
  59.8 2.6 %fusion.15 = f32[16,512]{1,0:T(8,128)} fusion(bf16[16,2048]{1,0:T(8,128)(2,1)S(1)} %reshape.26, bf16[512,2048]{0,1:T(8,128)(2,1)} %all-gather.2.cloned.1.call-done), kind=kOutput, calls=%fused_computation.16 | convolution fusion | flops 33554432 | bytes 2195456 | tf_op jit(solution)/shard_map/nk,qk->nq/dot_general | solution.py:30
  62.4 0.0 reduce-scatter.2.cloned.1.call-update
  62.4 17.9 %reduce-scatter.2.cloned.1.call-done = f32[16,128]{1,0:T(8,128)} async-done(((f32[16,512]{1,0:T(8,128)}), f32[16,128]{1,0:T(8,128)}) %reduce-scatter.2.cloned.1.call-update) | async-done | bytes 8208 | tf_op jit(solution)/shard_map/reduce_scatter | solution.py:36
  80.4 1.4 %compare_select_fusion = f32[16,128]{1,0:T(8,128)} fusion(f32[16,128]{1,0:T(8,128)} %reduce-scatter.2.cloned.1.call-done, s32[128]{0:T(128)S(1)} %dynamic_slice.3, s32[16]{0:T(128)S(1)} %iota_add_fusion), kind=kLoop, calls=%fused_computation.14 | loop fusion | flops 4096 | bytes 16960 | tf_op jit(solution)/shard_map/jit(_where)/select_n | solution.py:42
  (1 shorter events, 0.0 us)
Async XLA Ops:
  6.5 5.6 %copy-start = (bf16[2,16,32,1024]{3,2,1,0:T(8,128)(2,1)S(1)}, bf16[2,16,32,1024]{3,2,1,0:T(8,128)(2,1)}, u32[]{:S(2)}) copy-start(bf16[2,16,32,1024]{3,2,1,0:T(8,128)(2,1)} %param.7) | copy-start | bytes 6291460
  6.5 2.9 %copy-start.1 = (f32[2,32,32]{2,1,0:T(8,128)S(1)}, f32[2,32,32]{2,1,0:T(8,128)}, u32[]{:S(2)}) copy-start(f32[2,32,32]{2,1,0:T(8,128)} %param.11) | copy-start | bytes 24580
  6.5 53.3 %all-gather.2.cloned.1.call-start = ((), (), s32[]{:S(2)}) async-start(), calls=%async_computation.1 | async-start | bytes 2621440 | tf_op jit(solution)/shard_map/all_gather | solution.py:33
  8.1 4.0 %copy-start.2 = (s32[16]{0:T(128)S(1)}, s32[16]{0:T(128)}, u32[]{:S(2)}) copy-start(s32[16]{0:T(128)} %param.9) | copy-start | bytes 196
  12.0 68.3 %reduce-scatter.2.cloned.1.call-start = ((), (), s32[]{:S(2)}) async-start(), calls=%async_computation.2 | async-start | bytes 40960 | tf_op jit(solution)/shard_map/reduce_scatter | solution.py:36
Sparse Core Ops, SparseCore 0:
  12.1 47.6 all-gather.1
  62.5 17.7 reduce-scatter.1
where the time goes:
time: 90 us; the launch traced here: 88.6 us
  waiting for transfers between devices  62.3 us (69%)
  between operations  13.5 us (15%)
  matrix products  8.71 us (10%)
  local copies, waits for them, and re-layouts  2.62 us (3%)
  other arithmetic  1.45 us (2%)
    all_gather x1, waiting for transfers between devices, on_device(): lax.all_gather(precond, 'dp', axis=0, tiled=True)  44.3 us
    reduce_scatter x1, waiting for transfers between devices, on_device(): lax.psum_scatter(partial_value, ('layer', 'module'), scatter_dimension=1,...  17.9 us
    dot_general x1, matrix products, on_device(): jnp.einsum('nk,qk->nq', example_grads, lax.all_gather(precond, 'dp', axis...  2.59 us
    dot_general x1, matrix products, on_device(): jnp.einsum('qmac,mcd->qmad', half_done, inv_in, precision=lax.Precision.H...  2.51 us
    dot_general x1, matrix products, on_device(): jnp.einsum('mnot,mnit->nmoi', masked, train_acts, preferred_element_type=...  2.28 us
  transfers between devices with their start and end apart: 2, of which 2 were waited for; matrix products, arithmetic and copies ran while one was open for 4% of the time, Pallas kernels for 0%

commit v1 on v0

v1 whole, which is shorter than its diff:
```python
import functools

import jax
import jax.numpy as jnp
from jax import lax
from jax.experimental import pallas as pl
from jax.experimental.pallas import tpu as pltpu
from jax.sharding import PartitionSpec as P

MESH = pl.DeviceIdType.MESH
NT = (((1,), (1,)), ((), ()))
GROUP = 8


def iota(shape, dim):
    return lax.broadcasted_iota(jnp.int32, shape, dim)


def exact_dot(a, b):
    return jnp.dot(a, b, precision=lax.Precision.HIGHEST, preferred_element_type=jnp.float32)


def kernel(
    dp_size, layer_size, module_size,
    acts, grads, lengths, queries, inv_in, inv_out, ids,
    out,
    acts_v, grads_v, len_s, q_v, in_v, out_v, ids_v, q_flat, gathered, blocks, parts,
    load_sem, small_sem, send_sem, recv_sem, block_send, block_recv,
):
    mods, rows, seq = acts_v.shape
    rank = in_v.shape[1]
    ex = rows // rank
    width = rank * rank
    lm_size = layer_size * module_size
    groups = ex // GROUP
    grows = GROUP * rank
    local_q = q_v.shape[0]

    me = lax.axis_index("dp")
    lm = lax.axis_index("layer") * module_size + lax.axis_index("module")
    own_self = lm == me

    small = [
        pltpu.make_async_copy(lengths, len_s, small_sem.at[0]),
        pltpu.make_async_copy(inv_in, in_v, small_sem.at[1]),
        pltpu.make_async_copy(inv_out, out_v, small_sem.at[2]),
        pltpu.make_async_copy(ids, ids_v, small_sem.at[3]),
        pltpu.make_async_copy(queries, q_v, small_sem.at[4]),
    ]
    for copy in small[:4]:
        copy.start()
    loads = []
    for m in range(mods):
        for g in range(groups):
            part = pl.ds(g * grows, grows)
            k = m * groups + g
            pair = (
                pltpu.make_async_copy(grads.at[m, part], grads_v.at[m, part], load_sem.at[0, k]),
                pltpu.make_async_copy(acts.at[m, part], acts_v.at[m, part], load_sem.at[1, k]),
            )
            for copy in pair:
                copy.start()
            loads.append(pair)
    small[4].start()

    barrier = pltpu.get_barrier_semaphore()
    for k in range(1, dp_size):
        pl.semaphore_signal(
            barrier, inc=1, device_id={"dp": lax.rem(me + k, dp_size)}, device_id_type=MESH
        )
    for j in range(lm_size):
        @pl.when(jnp.logical_not(jnp.logical_and(own_self, lm == j)))
        def _(j=j):
            pl.semaphore_signal(
                barrier, inc=1,
                device_id={"dp": lm, "layer": j // module_size, "module": j % module_size},
                device_id_type=MESH,
            )

    for copy in small[:3]:
        copy.wait()
    spread_in = (iota((rank, 128), 0) == iota((rank, 128), 1) % rank).astype(jnp.float32)
    spread_out = (iota((rank, width), 0) == iota((rank, width), 1) // rank).astype(jnp.float32)
    block_diag = iota((grows, grows), 0) // rank == iota((grows, grows), 1) // rank
    positions = iota((1, seq), 1)
    right, left = [], []
    for m in range(mods):
        tiled = exact_dot(in_v[m], spread_in)
        high = tiled.astype(jnp.bfloat16)
        low = (tiled - high.astype(jnp.float32)).astype(jnp.bfloat16)
        both = jnp.concatenate([high, low], axis=1)
        right.append(jnp.concatenate([both] * GROUP, axis=0))
        left.append(exact_dot(out_v[m], spread_out))

    for m in range(mods):
        made = []
        for g in range(groups):
            for copy in loads[m * groups + g]:
                copy.wait()
            masked = []
            for n in range(GROUP):
                keep = (positions < len_s[g * GROUP + n]).astype(jnp.float32).astype(jnp.bfloat16)
                masked.append(grads_v[m, pl.ds(g * grows + n * rank, rank), :] * keep)
            outer = lax.dot_general(
                jnp.concatenate(masked, axis=0), acts_v[m, pl.ds(g * grows, grows), :], NT,
                preferred_element_type=jnp.float32,
            )
            diag = jnp.where(block_diag, outer, 0.0).astype(jnp.bfloat16)
            two = jnp.dot(diag, right[m], preferred_element_type=jnp.float32)
            half = (two[:, :128] + two[:, 128:]).reshape(GROUP, rank, 128)
            cols = []
            for c in range(width // 128):
                weight = left[m][:, c * 128:(c + 1) * 128]
                cols.append(jnp.sum(half * weight[None], axis=1))
            made.append(jnp.concatenate(cols, axis=1))
        gathered[m, me] = jnp.concatenate(made, axis=0).astype(jnp.bfloat16)
        if m == 0:
            pl.semaphore_wait(
                barrier, dp_size - 1 + dp_size - jnp.where(own_self, 1, 0)
            )
        for k in range(1, dp_size):
            to = lax.rem(me + k, dp_size)
            pltpu.make_async_remote_copy(
                src_ref=gathered.at[m, me], dst_ref=gathered.at[m, me],
                send_sem=send_sem.at[m, k], recv_sem=recv_sem.at[m, me],
                device_id={"dp": to}, device_id_type=MESH,
            ).start()

    small[3].wait()
    small[4].wait()
    q_flat[...] = q_v[...].reshape(local_q * mods, width)
    columns = local_q * mods
    parity = iota((1, columns), 1) % mods
    fold = (iota((columns, local_q), 0) // mods == iota((columns, local_q), 1)).astype(jnp.float32)

    def block_copy(slot, to):
        return pltpu.make_async_remote_copy(
            src_ref=blocks.at[slot], dst_ref=parts.at[lm],
            send_sem=block_send.at[slot], recv_sem=block_recv.at[lm],
            device_id={"dp": to, "layer": me // module_size, "module": me % module_size},
            device_id_type=MESH,
        )

    for k in range(dp_size):
        src = lax.rem(me + k, dp_size)
        total = None
        for m in range(mods):
            if k > 0:
                pltpu.make_async_remote_copy(
                    src_ref=gathered.at[m, src], dst_ref=gathered.at[m, src],
                    send_sem=send_sem.at[m, k], recv_sem=recv_sem.at[m, src],
                    device_id={"dp": src}, device_id_type=MESH,
                ).wait_recv()
            score = lax.dot_general(
                gathered[m, src], q_flat[...], NT, preferred_element_type=jnp.float32
            )
            total = score if total is None else jnp.where(parity == m, score, total)
        total = exact_dot(total, fold)
        if k == 0:
            @pl.when(own_self)
            def _():
                parts[lm] = total

            @pl.when(jnp.logical_not(own_self))
            def _():
                blocks[0] = total
                block_copy(0, src).start()
        else:
            blocks[k] = total
            block_copy(k, src).start()

    for j in range(lm_size):
        @pl.when(jnp.logical_not(jnp.logical_and(own_self, lm == j)))
        def _(j=j):
            pltpu.make_async_remote_copy(
                src_ref=blocks.at[0], dst_ref=parts.at[j],
                send_sem=block_send.at[0], recv_sem=block_recv.at[j],
                device_id={"dp": lm, "layer": j // module_size, "module": j % module_size},
                device_id_type=MESH,
            ).wait_recv()
    total = parts[0]
    for j in range(1, lm_size):
        total = total + parts[j]
    owned = ids_v[:, :local_q]
    for j in range(1, lm_size):
        owned = jnp.where(lm == j, ids_v[:, j * local_q:(j + 1) * local_q], owned)
    same = me * ex + iota((ex, local_q), 0) == owned
    out[...] = jnp.where(same, 0.0, total)

    for m in range(mods):
        for k in range(1, dp_size):
            pltpu.make_async_remote_copy(
                src_ref=gathered.at[m, me], dst_ref=gathered.at[m, me],
                send_sem=send_sem.at[m, k], recv_sem=recv_sem.at[m, me],
                device_id={"dp": lax.rem(me + k, dp_size)}, device_id_type=MESH,
            ).wait_send()
    for k in range(dp_size):
        if k == 0:
            @pl.when(jnp.logical_not(own_self))
            def _():
                block_copy(0, me).wait_send()
        else:
            block_copy(k, lax.rem(me + k, dp_size)).wait_send()


def on_device(sizes, train_acts, train_grads, lengths, query_grads, inv_in, inv_out, query_ids):
    dp_size, layer_size, module_size = sizes
    mods, ex, rank, seq = train_acts.shape
    local_q, _, width = query_grads.shape
    lm_size = layer_size * module_size
    rows = ex * rank
    chunks = mods * (ex // GROUP)
    anywhere = pl.BlockSpec(memory_space=pl.ANY)
    return pl.pallas_call(
        functools.partial(kernel, dp_size, layer_size, module_size),
        out_shape=jax.ShapeDtypeStruct((ex, local_q), jnp.float32),
        in_specs=[anywhere] * 7,
        out_specs=pl.BlockSpec(memory_space=pltpu.VMEM),
        scratch_shapes=[
            pltpu.VMEM((mods, rows, seq), jnp.bfloat16),
            pltpu.VMEM((mods, rows, seq), jnp.bfloat16),
            pltpu.SMEM((ex,), jnp.int32),
            pltpu.VMEM((local_q, mods, width), jnp.bfloat16),
            pltpu.VMEM((mods, rank, rank), jnp.float32),
            pltpu.VMEM((mods, rank, rank), jnp.float32),
            pltpu.VMEM((1, query_ids.shape[0]), jnp.int32),
            pltpu.VMEM((local_q * mods, width), jnp.bfloat16),
            pltpu.VMEM((mods, dp_size, ex, width), jnp.bfloat16),
            pltpu.VMEM((dp_size, ex, local_q), jnp.float32),
            pltpu.VMEM((lm_size, ex, local_q), jnp.float32),
            pltpu.SemaphoreType.DMA((2, chunks)),
            pltpu.SemaphoreType.DMA((5,)),
            pltpu.SemaphoreType.DMA((mods, dp_size)),
            pltpu.SemaphoreType.DMA((mods, dp_size)),
            pltpu.SemaphoreType.DMA((dp_size,)),
            pltpu.SemaphoreType.DMA((lm_size,)),
        ],
        compiler_params=pltpu.CompilerParams(
            collective_id=0, has_side_effects=True, vmem_limit_bytes=48 * 1024 * 1024
        ),
    )(
        train_acts.reshape(mods, rows, seq),
        train_grads.reshape(mods, rows, seq),
        lengths, query_grads, inv_in, inv_out,
        query_ids.reshape(1, -1),
    )


def solution(mesh):
    sizes = tuple(mesh.shape[name] for name in ("dp", "layer", "module"))
    assert sizes[0] == sizes[1] * sizes[2]
    return jax.shard_map(
        functools.partial(on_device, sizes),
        mesh=mesh,
        in_specs=(
            P(("layer", "module"), ("parts", "dp"), None, None),
            P(("layer", "module"), ("parts", "dp"), None, None),
            P(("parts", "dp")),
            P(("parts", "dp"), ("layer", "module"), None),
            P(("layer", "module"), None, None),
            P(("layer", "module"), None, None),
            P("parts"),
        ),
        out_specs=P(("parts", "dp"), ("layer", "module")),
        check_vma=False,
    )
```

time: 90 us -> 26 us (0.29); the launches traced: 88.6 us -> 25.6 us
  waiting for transfers between devices: 62.3 us -> 0 us
  Pallas kernels: 0 us -> 18 us
  between operations: 13.5 us -> 0.02 us
  matrix products: 8.71 us -> 0 us
  local copies, waits for them, and re-layouts: 2.62 us -> 7.67 us
  other arithmetic: 1.45 us -> 0 us
    all_gather x1 -> x0, waiting for transfers between devices: 44.3 us -> none  [on_device(): lax.all_gather(precond, 'dp', axis=0, tiled=True)]
    pallas_call x0 -> x1, Pallas kernels: none -> 18 us  [on_device(): pl.pallas_call(functools.partial(kernel, dp_size, layer_size, module_size...]
    reduce_scatter x1 -> x0, waiting for transfers between devices: 17.9 us -> none  [on_device(): lax.psum_scatter(partial_value, ('layer', 'module'), scatter_dimension=1,...]
    dot_general x4 -> x0, matrix products: 8.71 us -> none  [the longest x1 2.59 us: on_device(): jnp.einsum('nk,qk->nq', example_grads, lax.all_gather(precond, 'dp', axis...]
    unnamed x7 -> x15, local copies, waits for them, and re-layouts: 1.57 us -> 7.67 us
    select_n x1 -> x0, other arithmetic: 1.37 us -> none  [on_device(): return jnp.where(same, jnp.zeros_like(owned_scores), owned_scores)]
  transfers between devices with their start and end apart: 2 -> 0, of which waited for: 2 -> 0; matrix products, arithmetic and copies ran while one was open for 4% -> 0% of each run, Pallas kernels for 0% -> 0%
where the time goes in v1:
time: 26 us; the launch traced here: 25.6 us
  Pallas kernels  18 us (69%)
  local copies, waits for them, and re-layouts  7.67 us (30%)
    pallas_call x1, Pallas kernels, on_device(): pl.pallas_call(functools.partial(kernel, dp_size, layer_size, module_size...  18 us
    unnamed x15, local copies, waits for them, and re-layouts  7.67 us

profile of v1, /device:TPU:1, one launch (start us, length us, event | category | flops | bytes accessed | tf_op | source)
XLA Modules:
  0.0 25.6 jit_solution(1939023844792994657)
XLA Ops:
  0.0 0.0 copy-start
  0.0 1.6 %copy-done = bf16[2,16,32,1024]{3,2,1,0:T(8,128)(2,1)S(1)} copy-done((bf16[2,16,32,1024]{3,2,1,0:T(8,128)(2,1)S(1)}, bf16[2,16,32,1024]{3,2,1,0:T(8,128)(2,1)}, u32[]{:S(2)}) %copy-start) | copy-done | bytes 2097176
  1.6 0.0 copy-start.1
  1.6 1.6 %copy-done.1 = bf16[2,16,32,1024]{3,2,1,0:T(8,128)(2,1)S(1)} copy-done((bf16[2,16,32,1024]{3,2,1,0:T(8,128)(2,1)S(1)}, bf16[2,16,32,1024]{3,2,1,0:T(8,128)(2,1)}, u32[]{:S(2)}) %copy-start.1) | copy-done | bytes 2097176
  3.2 0.0 copy-start.2
  3.2 1.0 %copy-done.2 = bf16[128,2,1024]{2,1,0:T(2,128)(2,1)S(1)} copy-done((bf16[128,2,1024]{2,1,0:T(2,128)(2,1)S(1)}, bf16[128,2,1024]{2,1,0:T(2,128)(2,1)}, u32[]{:S(2)}) %copy-start.2) | copy-done | bytes 524312
  4.2 0.0 copy-start.3
  4.2 0.8 %copy-done.3 = f32[2,32,32]{2,1,0:T(8,128)S(1)} copy-done((f32[2,32,32]{2,1,0:T(8,128)S(1)}, f32[2,32,32]{2,1,0:T(8,128)}, u32[]{:S(2)}) %copy-start.3) | copy-done | bytes 8216
  5.0 0.0 copy-start.4
  5.0 0.8 %copy-done.4 = f32[2,32,32]{2,1,0:T(8,128)S(1)} copy-done((f32[2,32,32]{2,1,0:T(8,128)S(1)}, f32[2,32,32]{2,1,0:T(8,128)}, u32[]{:S(2)}) %copy-start.4) | copy-done | bytes 8216
  5.7 0.0 copy-start.5
  5.7 0.7 %copy-done.5 = s32[512]{0:T(512)S(1)} copy-done((s32[512]{0:T(512)S(1)}, s32[512]{0:T(512)}, u32[]{:S(2)}) %copy-start.5) | copy-done | bytes 2072
  6.4 0.0 copy-start.6
  6.4 0.7 %copy-done.6 = s32[16]{0:T(128)S(1)} copy-done((s32[16]{0:T(128)S(1)}, s32[16]{0:T(128)}, u32[]{:S(2)}) %copy-start.6) | copy-done | bytes 88
  7.1 18.0 %shard_map.73 = f32[16,128]{1,0:T(8,128)S(1)} custom-call(bf16[2,512,1024]{2,1,0:T(8,128)(2,1)S(1)} %bitcast.3, bf16[2,512,1024]{2,1,0:T(8,128)(2,1)S(1)} %bitcast.4, s32[16]{0:T(128)S(1)} %copy-done.6, bf16[128,2,1024]{2,1,0:T(2,128)(2,1)S(1)} %copy-done.2, f32[2,32,32]{2,1,0:T(8,128)S(1)} %copy-done.3, f32[2,32,32]{2,1,0:T(8,128)S(1)} %copy-done.4, ...), custom_call_target="tpu_custom_call" | custom-call | tf_op jit(solution)/shard_map/pallas_call | solution.py:214
  25.0 0.6 %copy.9 = f32[16,128]{1,0:T(8,128)} copy(f32[16,128]{1,0:T(8,128)S(1)} %shard_map.73) | data formatting | bytes 16384
Async XLA Ops:
  0.0 1.6 %copy-start = (bf16[2,16,32,1024]{3,2,1,0:T(8,128)(2,1)S(1)}, bf16[2,16,32,1024]{3,2,1,0:T(8,128)(2,1)}, u32[]{:S(2)}) copy-start(bf16[2,16,32,1024]{3,2,1,0:T(8,128)(2,1)} %param.7) | copy-start | bytes 6291460
  1.6 1.6 %copy-start.1 = (bf16[2,16,32,1024]{3,2,1,0:T(8,128)(2,1)S(1)}, bf16[2,16,32,1024]{3,2,1,0:T(8,128)(2,1)}, u32[]{:S(2)}) copy-start(bf16[2,16,32,1024]{3,2,1,0:T(8,128)(2,1)} %param.8) | copy-start | bytes 6291460
  3.2 1.0 %copy-start.2 = (bf16[128,2,1024]{2,1,0:T(2,128)(2,1)S(1)}, bf16[128,2,1024]{2,1,0:T(2,128)(2,1)}, u32[]{:S(2)}) copy-start(bf16[128,2,1024]{2,1,0:T(2,128)(2,1)} %queries.1) | copy-start | bytes 1572868
  4.2 0.8 %copy-start.3 = (f32[2,32,32]{2,1,0:T(8,128)S(1)}, f32[2,32,32]{2,1,0:T(8,128)}, u32[]{:S(2)}) copy-start(f32[2,32,32]{2,1,0:T(8,128)} %inv_in.1) | copy-start | bytes 24580
  5.0 0.8 %copy-start.4 = (f32[2,32,32]{2,1,0:T(8,128)S(1)}, f32[2,32,32]{2,1,0:T(8,128)}, u32[]{:S(2)}) copy-start(f32[2,32,32]{2,1,0:T(8,128)} %inv_out.1) | copy-start | bytes 24580
  5.7 0.7 %copy-start.5 = (s32[512]{0:T(512)S(1)}, s32[512]{0:T(512)}, u32[]{:S(2)}) copy-start(s32[512]{0:T(512)} %param.13) | copy-start | bytes 6148
  6.4 0.7 %copy-start.6 = (s32[16]{0:T(128)S(1)}, s32[16]{0:T(128)}, u32[]{:S(2)}) copy-start(s32[16]{0:T(128)} %lengths.1) | copy-start | bytes 196

commit v2 on v1

v2 whole, which is shorter than its diff:
```python
import functools

import jax
import jax.numpy as jnp
from jax import lax
from jax.experimental import pallas as pl
from jax.experimental.pallas import tpu as pltpu
from jax.sharding import PartitionSpec as P

MESH = pl.DeviceIdType.MESH
NT = (((1,), (1,)), ((), ()))
GROUP = 8


def iota(shape, dim):
    return lax.broadcasted_iota(jnp.int32, shape, dim)


def plain_dot(a, b):
    return jnp.dot(a, b, preferred_element_type=jnp.float32)


def terms(x):
    high = x.astype(jnp.bfloat16)
    rest = x - high.astype(jnp.float32)
    middle = rest.astype(jnp.bfloat16)
    return high, middle, (rest - middle.astype(jnp.float32)).astype(jnp.bfloat16)


def kernel(
    dp_size, layer_size, module_size,
    acts, grads, lengths, queries, inv_in, inv_out, ids,
    out,
    acts_v, grads_v, len_s, q_v, in_v, out_v, ids_v, right, left, q_t, gathered, blocks, parts,
    load_sem, small_sem, send_sem, recv_sem, block_send, block_recv,
):
    mods, rows, seq = acts_v.shape
    rank = in_v.shape[1]
    ex = rows // rank
    width = rank * rank
    lm_size = layer_size * module_size
    groups = ex // GROUP
    grows = GROUP * rank
    local_q = q_v.shape[0]

    me = lax.axis_index("dp")
    lm = lax.axis_index("layer") * module_size + lax.axis_index("module")
    own_self = lm == me
    upper = 2 * me >= dp_size

    def peer(i):
        down = dp_size - 1 - i
        up = jnp.where(me <= i, i + 1, i)
        return jnp.where(upper, up, jnp.where(down <= me, down - 1, down))

    small = [
        pltpu.make_async_copy(lengths, len_s, small_sem.at[0]),
        pltpu.make_async_copy(inv_in, in_v, small_sem.at[1]),
        pltpu.make_async_copy(inv_out, out_v, small_sem.at[2]),
        pltpu.make_async_copy(ids, ids_v, small_sem.at[3]),
        pltpu.make_async_copy(queries, q_v, small_sem.at[4]),
    ]
    for copy in small[:4]:
        copy.start()

    def load_copy(pair, m, g):
        part = pl.ds(pl.multiple_of(g * grows, grows), grows)
        source, target = ((grads, grads_v), (acts, acts_v))[pair]
        return pltpu.make_async_copy(
            source.at[m, part], target.at[m, part], load_sem.at[pair, m, g]
        )

    for m in range(mods):
        for g in range(groups):
            for pair in range(2):
                load_copy(pair, m, g).start()
    small[4].start()

    barrier = pltpu.get_barrier_semaphore()
    for k in range(1, dp_size):
        pl.semaphore_signal(
            barrier, inc=1, device_id={"dp": lax.rem(me + k, dp_size)}, device_id_type=MESH
        )
    for j in range(lm_size):
        @pl.when(jnp.logical_not(jnp.logical_and(own_self, lm == j)))
        def _(j=j):
            pl.semaphore_signal(
                barrier, inc=1,
                device_id={"dp": lm, "layer": j // module_size, "module": j % module_size},
                device_id_type=MESH,
            )

    half = width // 2

    def rows_copy(m, g, owner, slot, to):
        place = gathered.at[m, owner, pl.ds(pl.multiple_of(g * 2 * GROUP, 2 * GROUP), 2 * GROUP)]
        return pltpu.make_async_remote_copy(
            src_ref=place, dst_ref=place,
            send_sem=send_sem.at[m, g, slot], recv_sem=recv_sem.at[m, g, owner],
            device_id={"dp": to}, device_id_type=MESH,
        )

    def loop(count, body):
        def step(i, carry):
            body(i)
            return carry

        lax.fori_loop(0, count, step, 0)

    for copy in small[:3]:
        copy.wait()
    spread_in = (iota((rank, 128), 0) == iota((rank, 128), 1) % rank).astype(jnp.bfloat16)
    spread_out = (iota((rank, width), 0) == iota((rank, width), 1) // rank).astype(jnp.bfloat16)
    positions = iota((1, seq), 1)

    def set_up(m):
        high, low, _ = terms(in_v[m])
        both = jnp.concatenate([plain_dot(high, spread_in), plain_dot(low, spread_in)], axis=1)
        right[m] = jnp.concatenate([both.astype(jnp.bfloat16)] * GROUP, axis=0)
        left[m] = sum(plain_dot(term, spread_out) for term in terms(out_v[m]))

    loop(mods, set_up)

    def chunk(c):
        m, g = c // groups, c % groups
        start = pl.multiple_of(g * grows, grows)
        for pair in range(2):
            load_copy(pair, m, g).wait()
        masked = []
        for n in range(GROUP):
            keep = (positions < len_s[g * GROUP + n]).astype(jnp.float32).astype(jnp.bfloat16)
            masked.append(grads_v[m, pl.ds(start + n * rank, rank), :] * keep)
        outer = lax.dot_general(
            jnp.concatenate(masked, axis=0), acts_v[m, pl.ds(start, grows), :], NT,
            preferred_element_type=jnp.float32,
        )
        block_diag = iota((grows, grows), 0) // rank == iota((grows, grows), 1) // rank
        diag = jnp.where(block_diag, outer, 0.0).astype(jnp.bfloat16)
        two = plain_dot(diag, right[m])
        one = (two[:, :128] + two[:, 128:]).reshape(GROUP, rank, 128)
        cols = []
        for col in range(width // 128):
            weight = left[m, :, col * 128:(col + 1) * 128]
            cols.append(jnp.sum(one * weight[None], axis=1))
        made = jnp.concatenate(cols, axis=1)
        gathered[m, me, pl.ds(pl.multiple_of(g * 2 * GROUP, 2 * GROUP), 2 * GROUP)] = (
            jnp.concatenate([made[:, :half], made[:, half:]], axis=0).astype(jnp.bfloat16)
        )

        @pl.when(c == 0)
        def _():
            pl.semaphore_wait(barrier, dp_size - 1 + dp_size - jnp.where(own_self, 1, 0))

        for i in range(dp_size - 1):
            rows_copy(m, g, me, i, peer(i)).start()

    loop(mods * groups, chunk)

    small[3].wait()
    small[4].wait()
    columns = local_q * mods

    def prepare(m):
        pick = iota((local_q, columns), 1) == iota((local_q, columns), 0) * mods + m
        chosen = plain_dot(pick.astype(jnp.bfloat16), q_v[...].reshape(columns, width))
        q_t[m] = chosen.T.astype(jnp.bfloat16)

    loop(mods, prepare)

    def block_copy(slot, sender, to):
        return pltpu.make_async_remote_copy(
            src_ref=blocks.at[slot], dst_ref=parts.at[sender],
            send_sem=block_send.at[slot], recv_sem=block_recv.at[sender],
            device_id={"dp": to, "layer": me // module_size, "module": me % module_size},
            device_id_type=MESH,
        )

    def source(k):
        return jnp.where(k == 0, me, peer(dp_size - 1 - k))

    def score(k):
        src = source(k)

        @pl.when(k > 0)
        def _():
            for m in range(mods):
                for g in range(groups):
                    rows_copy(m, g, src, 0, src).wait_recv()

        sides = [
            sum(plain_dot(gathered[m, src], q_t[m, side]) for m in range(mods))
            for side in (pl.ds(0, half), pl.ds(half, half))
        ]
        total = jnp.concatenate([
            sides[0][2 * g * GROUP:(2 * g + 1) * GROUP]
            + sides[1][(2 * g + 1) * GROUP:(2 * g + 2) * GROUP]
            for g in range(groups)
        ], axis=0)
        stays = jnp.logical_and(own_self, k == 0)

        @pl.when(stays)
        def _():
            parts[lm] = total

        @pl.when(jnp.logical_not(stays))
        def _():
            blocks[k] = total
            block_copy(k, lm, src).start()

    loop(dp_size, score)

    def collect(j):
        @pl.when(jnp.logical_not(jnp.logical_and(own_self, lm == j)))
        def _():
            block_copy(0, j, lm).wait_recv()

    loop(lm_size, collect)
    total = parts[0]
    for j in range(1, lm_size):
        total = total + parts[j]
    owned = ids_v[:, :local_q]
    for j in range(1, lm_size):
        owned = jnp.where(lm == j, ids_v[:, j * local_q:(j + 1) * local_q], owned)
    same = me * ex + iota((ex, local_q), 0) == owned
    out[...] = jnp.where(same, 0.0, total)

    def sent(i):
        for m in range(mods):
            for g in range(groups):
                rows_copy(m, g, me, i, peer(i)).wait_send()

    loop(dp_size - 1, sent)

    def block_sent(k):
        @pl.when(jnp.logical_not(jnp.logical_and(own_self, k == 0)))
        def _():
            block_copy(k, lm, source(k)).wait_send()

    loop(dp_size, block_sent)


def on_device(sizes, train_acts, train_grads, lengths, query_grads, inv_in, inv_out, query_ids):
    dp_size, layer_size, module_size = sizes
    mods, ex, rank, seq = train_acts.shape
    local_q, _, width = query_grads.shape
    lm_size = layer_size * module_size
    rows = ex * rank
    anywhere = pl.BlockSpec(memory_space=pltpu.HBM)
    return pl.pallas_call(
        functools.partial(kernel, dp_size, layer_size, module_size),
        out_shape=jax.ShapeDtypeStruct((ex, local_q), jnp.float32),
        in_specs=[anywhere] * 7,
        out_specs=pl.BlockSpec(memory_space=pltpu.VMEM),
        scratch_shapes=[
            pltpu.VMEM((mods, rows, seq), jnp.bfloat16),
            pltpu.VMEM((mods, rows, seq), jnp.bfloat16),
            pltpu.SMEM((ex,), jnp.int32),
            pltpu.VMEM((local_q, mods, width), jnp.bfloat16),
            pltpu.VMEM((mods, rank, rank), jnp.float32),
            pltpu.VMEM((mods, rank, rank), jnp.float32),
            pltpu.VMEM((1, query_ids.shape[0]), jnp.int32),
            pltpu.VMEM((mods, GROUP * rank, 256), jnp.bfloat16),
            pltpu.VMEM((mods, rank, width), jnp.float32),
            pltpu.VMEM((mods, width, local_q), jnp.bfloat16),
            pltpu.VMEM((mods, dp_size, 2 * ex, width // 2), jnp.bfloat16),
            pltpu.VMEM((dp_size, ex, local_q), jnp.float32),
            pltpu.VMEM((lm_size, ex, local_q), jnp.float32),
            pltpu.SemaphoreType.DMA((2, mods, ex // GROUP)),
            pltpu.SemaphoreType.DMA((5,)),
            pltpu.SemaphoreType.DMA((mods, ex // GROUP, dp_size)),
            pltpu.SemaphoreType.DMA((mods, ex // GROUP, dp_size)),
            pltpu.SemaphoreType.DMA((dp_size,)),
            pltpu.SemaphoreType.DMA((lm_size,)),
        ],
        compiler_params=pltpu.CompilerParams(
            collective_id=0, has_side_effects=True, vmem_limit_bytes=60 * 1024 * 1024
        ),
    )(
        train_acts.reshape(mods, rows, seq),
        train_grads.reshape(mods, rows, seq),
        lengths, query_grads, inv_in, inv_out,
        query_ids.reshape(1, -1),
    )


def solution(mesh):
    sizes = tuple(mesh.shape[name] for name in ("dp", "layer", "module"))
    assert sizes[0] == sizes[1] * sizes[2]
    return jax.shard_map(
        functools.partial(on_device, sizes),
        mesh=mesh,
        in_specs=(
            P(("layer", "module"), ("parts", "dp"), None, None),
            P(("layer", "module"), ("parts", "dp"), None, None),
            P(("parts", "dp")),
            P(("parts", "dp"), ("layer", "module"), None),
            P(("layer", "module"), None, None),
            P(("layer", "module"), None, None),
            P("parts"),
        ),
        out_specs=P(("parts", "dp"), ("layer", "module")),
        check_vma=False,
    )
```

time: 26 us -> 17.7 us (0.68)
  the two profiles are of different devices: /device:TPU:1 before, /device:TPU:0 now
where the time goes in v2:
time: 17.7 us; the launch traced here: 17.5 us
  Pallas kernels  16.2 us (92%)
  local copies, waits for them, and re-layouts  1.3 us (7%)
    pallas_call x1, Pallas kernels, on_device(): pl.pallas_call(functools.partial(kernel, dp_size, layer_size, module_size...  16.2 us
    unnamed x1, local copies, waits for them, and re-layouts  1.3 us

profile of v2, /device:TPU:0, one launch (start us, length us, event | category | flops | bytes accessed | tf_op | source)
XLA Modules:
  0.0 17.5 jit_solution(7654924891178801100)
XLA Ops:
  0.0 16.2 %shard_map.73 = f32[16,128]{1,0:T(8,128)} custom-call(bf16[2,512,1024]{2,1,0:T(8,128)(2,1)} %bitcast.3, bf16[2,512,1024]{2,1,0:T(8,128)(2,1)} %bitcast.4, s32[16]{0:T(128)} %lengths.1, bf16[128,2,1024]{2,1,0:T(2,128)(2,1)} %queries.1, f32[2,32,32]{2,1,0:T(8,128)} %inv_in.1, f32[2,32,32]{2,1,0:T(8,128)} %inv_out.1, s32[1,512]{1,0:T(1,128)} %bitcast.5), custom_call_target="tpu_custom_call" | custom-call | tf_op jit(solution)/shard_map/pallas_call | solution.py:249
  16.2 1.3 %copy.9 = f32[16,128]{1,0:T(8,128)} copy(f32[16,128]{1,0:T(8,128)} %shard_map.73) | data formatting | bytes 16384

commit v3 on v2

--- a/solution.py
+++ b/solution.py
@@ -53,29 +53,6 @@
         up = jnp.where(me <= i, i + 1, i)
         return jnp.where(upper, up, jnp.where(down <= me, down - 1, down))
 
-    small = [
-        pltpu.make_async_copy(lengths, len_s, small_sem.at[0]),
-        pltpu.make_async_copy(inv_in, in_v, small_sem.at[1]),
-        pltpu.make_async_copy(inv_out, out_v, small_sem.at[2]),
-        pltpu.make_async_copy(ids, ids_v, small_sem.at[3]),
-        pltpu.make_async_copy(queries, q_v, small_sem.at[4]),
-    ]
-    for copy in small[:4]:
-        copy.start()
-
-    def load_copy(pair, m, g):
-        part = pl.ds(pl.multiple_of(g * grows, grows), grows)
-        source, target = ((grads, grads_v), (acts, acts_v))[pair]
-        return pltpu.make_async_copy(
-            source.at[m, part], target.at[m, part], load_sem.at[pair, m, g]
-        )
-
-    for m in range(mods):
-        for g in range(groups):
-            for pair in range(2):
-                load_copy(pair, m, g).start()
-    small[4].start()
-
     barrier = pltpu.get_barrier_semaphore()
     for k in range(1, dp_size):
         pl.semaphore_signal(
@@ -92,11 +69,11 @@
 
     half = width // 2
 
-    def rows_copy(m, g, owner, slot, to):
-        place = gathered.at[m, owner, pl.ds(pl.multiple_of(g * 2 * GROUP, 2 * GROUP), 2 * GROUP)]
+    def rows_copy(m, owner, slot, to):
+        place = gathered.at[m, owner]
         return pltpu.make_async_remote_copy(
             src_ref=place, dst_ref=place,
-            send_sem=send_sem.at[m, g, slot], recv_sem=recv_sem.at[m, g, owner],
+            send_sem=send_sem.at[m, slot], recv_sem=recv_sem.at[m, owner],
             device_id={"dp": to}, device_id_type=MESH,
         )
 
@@ -106,6 +83,30 @@
             return carry
 
         lax.fori_loop(0, count, step, 0)
+
+    small = [
+        pltpu.make_async_copy(lengths, len_s, small_sem.at[0]),
+        pltpu.make_async_copy(inv_in, in_v, small_sem.at[1]),
+        pltpu.make_async_copy(inv_out, out_v, small_sem.at[2]),
+        pltpu.make_async_copy(ids, ids_v, small_sem.at[3]),
+        pltpu.make_async_copy(queries, q_v, small_sem.at[4]),
+    ]
+
+    def load_copy(pair, m, g):
+        part = pl.ds(pl.multiple_of(g * grows, grows), grows)
+        source, target = ((grads, grads_v), (acts, acts_v))[pair]
+        return pltpu.make_async_copy(
+            source.at[m, part], target.at[m, part], load_sem.at[pair, m, g]
+        )
+
+    def load(m):
+        for g in range(groups):
+            for pair in range(2):
+                load_copy(pair, m, g).start()
+
+    load(0)
+    for copy in small[:4]:
+        copy.start()
 
     for copy in small[:3]:
         copy.wait()
@@ -119,13 +120,15 @@
         right[m] = jnp.concatenate([both.astype(jnp.bfloat16)] * GROUP, axis=0)
         left[m] = sum(plain_dot(term, spread_out) for term in terms(out_v[m]))
 
+    for m in range(1, mods):
+        load(m)
+
     loop(mods, set_up)
 
-    def chunk(c):
-        m, g = c // groups, c % groups
-        start = pl.multiple_of(g * grows, grows)
-        for pair in range(2):
-            load_copy(pair, m, g).wait()
+    block_diag = iota((grows, grows), 0) // rank == iota((grows, grows), 1) // rank
+
+    def rows_of(m, g):
+        start = g * grows
         masked = []
         for n in range(GROUP):
             keep = (positions < len_s[g * GROUP + n]).astype(jnp.float32).astype(jnp.bfloat16)
@@ -134,7 +137,6 @@
             jnp.concatenate(masked, axis=0), acts_v[m, pl.ds(start, grows), :], NT,
             preferred_element_type=jnp.float32,
         )
-        block_diag = iota((grows, grows), 0) // rank == iota((grows, grows), 1) // rank
         diag = jnp.where(block_diag, outer, 0.0).astype(jnp.bfloat16)
         two = plain_dot(diag, right[m])
         one = (two[:, :128] + two[:, 128:]).reshape(GROUP, rank, 128)
@@ -143,18 +145,23 @@
             weight = left[m, :, col * 128:(col + 1) * 128]
             cols.append(jnp.sum(one * weight[None], axis=1))
         made = jnp.concatenate(cols, axis=1)
-        gathered[m, me, pl.ds(pl.multiple_of(g * 2 * GROUP, 2 * GROUP), 2 * GROUP)] = (
-            jnp.concatenate([made[:, :half], made[:, half:]], axis=0).astype(jnp.bfloat16)
-        )
-
-        @pl.when(c == 0)
-        def _():
+        return jnp.concatenate([made[:, :half], made[:, half:]], axis=0).astype(jnp.bfloat16)
+
+    def module_rows(m):
+        for g in range(groups):
+            for pair in range(2):
+                load_copy(pair, m, g).wait()
+        gathered[m, me] = jnp.concatenate([rows_of(m, g) for g in range(groups)], axis=0)
+
+        @pl.when(m == 0)
+        def _():
+            small[4].start()
             pl.semaphore_wait(barrier, dp_size - 1 + dp_size - jnp.where(own_self, 1, 0))
 
         for i in range(dp_size - 1):
-            rows_copy(m, g, me, i, peer(i)).start()
-
-    loop(mods * groups, chunk)
+            rows_copy(m, me, i, peer(i)).start()
+
+    loop(mods, module_rows)
 
     small[3].wait()
     small[4].wait()
@@ -184,8 +191,7 @@
         @pl.when(k > 0)
         def _():
             for m in range(mods):
-                for g in range(groups):
-                    rows_copy(m, g, src, 0, src).wait_recv()
+                rows_copy(m, src, 0, src).wait_recv()
 
         sides = [
             sum(plain_dot(gathered[m, src], q_t[m, side]) for m in range(mods))
@@ -226,8 +232,7 @@
 
     def sent(i):
         for m in range(mods):
-            for g in range(groups):
-                rows_copy(m, g, me, i, peer(i)).wait_send()
+            rows_copy(m, me, i, peer(i)).wait_send()
 
     loop(dp_size - 1, sent)
 
@@ -267,8 +272,8 @@
             pltpu.VMEM((lm_size, ex, local_q), jnp.float32),
             pltpu.SemaphoreType.DMA((2, mods, ex // GROUP)),
             pltpu.SemaphoreType.DMA((5,)),
-            pltpu.SemaphoreType.DMA((mods, ex // GROUP, dp_size)),
-            pltpu.SemaphoreType.DMA((mods, ex // GROUP, dp_size)),
+            pltpu.SemaphoreType.DMA((mods, dp_size)),
+            pltpu.SemaphoreType.DMA((mods, dp_size)),
             pltpu.SemaphoreType.DMA((dp_size,)),
             pltpu.SemaphoreType.DMA((lm_size,)),
         ],

time: 17.7 us -> 17.3 us (0.977)
  the two profiles are of different devices: /device:TPU:0 before, /device:TPU:7 now
where the time goes in v3:
time: 17.3 us; the launch traced here: 17.2 us
  Pallas kernels  15.8 us (91%)
  local copies, waits for them, and re-layouts  1.3 us (8%)
    pallas_call x1, Pallas kernels, on_device(): pl.pallas_call(functools.partial(kernel, dp_size, layer_size, module_size...  15.8 us
    unnamed x1, local copies, waits for them, and re-layouts  1.3 us

profile of v3, /device:TPU:7, one launch (start us, length us, event | category | flops | bytes accessed | tf_op | source)
XLA Modules:
  0.0 17.2 jit_solution(14722637928082534118)
XLA Ops:
  0.0 15.8 %shard_map.73 = f32[16,128]{1,0:T(8,128)} custom-call(bf16[2,512,1024]{2,1,0:T(8,128)(2,1)} %bitcast.3, bf16[2,512,1024]{2,1,0:T(8,128)(2,1)} %bitcast.4, s32[16]{0:T(128)} %lengths.1, bf16[128,2,1024]{2,1,0:T(2,128)(2,1)} %queries.1, f32[2,32,32]{2,1,0:T(8,128)} %inv_in.1, f32[2,32,32]{2,1,0:T(8,128)} %inv_out.1, s32[1,512]{1,0:T(1,128)} %bitcast.5), custom_call_target="tpu_custom_call" | custom-call | tf_op jit(solution)/shard_map/pallas_call | solution.py:254
  15.9 1.3 %copy.9 = f32[16,128]{1,0:T(8,128)} copy(f32[16,128]{1,0:T(8,128)} %shard_map.73) | data formatting | bytes 16384

commit v4 on v3

--- a/solution.py
+++ b/solution.py
@@ -31,7 +31,7 @@
     dp_size, layer_size, module_size,
     acts, grads, lengths, queries, inv_in, inv_out, ids,
     out,
-    acts_v, grads_v, len_s, q_v, in_v, out_v, ids_v, right, left, q_t, gathered, blocks, parts,
+    acts_v, grads_v, len_s, q_v, in_v, out_v, ids_v, right, left, q_t, held, gathered, blocks, parts,
     load_sem, small_sem, send_sem, recv_sem, block_send, block_recv,
 ):
     mods, rows, seq = acts_v.shape
@@ -185,17 +185,32 @@
     def source(k):
         return jnp.where(k == 0, me, peer(dp_size - 1 - k))
 
+    def early(k):
+        src = source(k)
+
+        @pl.when(k > 0)
+        def _():
+            for m in range(mods - 1):
+                rows_copy(m, src, 0, src).wait_recv()
+
+        for side in range(2):
+            held[side, k] = sum(
+                plain_dot(gathered[m, src], q_t[m, pl.ds(side * half, half)])
+                for m in range(mods - 1)
+            )
+
+    loop(dp_size, early)
+
     def score(k):
         src = source(k)
 
         @pl.when(k > 0)
         def _():
-            for m in range(mods):
-                rows_copy(m, src, 0, src).wait_recv()
+            rows_copy(mods - 1, src, 0, src).wait_recv()
 
         sides = [
-            sum(plain_dot(gathered[m, src], q_t[m, side]) for m in range(mods))
-            for side in (pl.ds(0, half), pl.ds(half, half))
+            held[side, k] + plain_dot(gathered[mods - 1, src], q_t[mods - 1, pl.ds(side * half, half)])
+            for side in range(2)
         ]
         total = jnp.concatenate([
             sides[0][2 * g * GROUP:(2 * g + 1) * GROUP]
@@ -267,6 +282,7 @@
             pltpu.VMEM((mods, GROUP * rank, 256), jnp.bfloat16),
             pltpu.VMEM((mods, rank, width), jnp.float32),
             pltpu.VMEM((mods, width, local_q), jnp.bfloat16),
+            pltpu.VMEM((2, dp_size, 2 * ex, local_q), jnp.float32),
             pltpu.VMEM((mods, dp_size, 2 * ex, width // 2), jnp.bfloat16),
             pltpu.VMEM((dp_size, ex, local_q), jnp.float32),
             pltpu.VMEM((lm_size, ex, local_q), jnp.float32),

time: 17.3 us -> 17.4 us (level)
  the two profiles are of different devices: /device:TPU:7 before, /device:TPU:1 now
where the time goes in v4:
time: 17.4 us; the launch traced here: 17.2 us
  Pallas kernels  15.9 us (91%)
  local copies, waits for them, and re-layouts  1.3 us (7%)
    pallas_call x1, Pallas kernels, on_device(): pl.pallas_call(functools.partial(kernel, dp_size, layer_size, module_size...  15.9 us
    unnamed x1, local copies, waits for them, and re-layouts  1.3 us

profile of v4, /device:TPU:1, one launch (start us, length us, event | category | flops | bytes accessed | tf_op | source)
XLA Modules:
  0.0 17.2 jit_solution(1798784857127223589)
XLA Ops:
  0.0 15.9 %shard_map.73 = f32[16,128]{1,0:T(8,128)} custom-call(bf16[2,512,1024]{2,1,0:T(8,128)(2,1)} %bitcast.3, bf16[2,512,1024]{2,1,0:T(8,128)(2,1)} %bitcast.4, s32[16]{0:T(128)} %lengths.1, bf16[128,2,1024]{2,1,0:T(2,128)(2,1)} %queries.1, f32[2,32,32]{2,1,0:T(8,128)} %inv_in.1, f32[2,32,32]{2,1,0:T(8,128)} %inv_out.1, s32[1,512]{1,0:T(1,128)} %bitcast.5), custom_call_target="tpu_custom_call" | custom-call | tf_op jit(solution)/shard_map/pallas_call | solution.py:269
  15.9 1.3 %copy.9 = f32[16,128]{1,0:T(8,128)} copy(f32[16,128]{1,0:T(8,128)} %shard_map.73) | data formatting | bytes 16384
